TPU v7x, 256 devices: a whole 4x4x8 slice. The times are simulated.
256 devices in a mesh: ex: 32 (over z, x_hi, core), blk: 8 (over x_lo, y).
Axes of the slice: x: 4 (x_hi: 2, x_lo: 2; x = x_hi * 2 + x_lo), y: 4, z: 8, core: 2. Of those that a mesh axis runs over, the one named last changes fastest.
Arguments:
- acts: bfloat16 [8, 128, 64, 4096], P('blk', 'ex'), may hold values from -6 to 6
- out_grads: bfloat16 [8, 128, 64, 14336], P('blk', 'ex'), may hold values from -6 to 6
- proj_in: bfloat16 [8, 64, 4096], P('blk'), may hold values from -0.09375 to 0.09375
- proj_out: bfloat16 [8, 64, 14336], P('blk'), may hold values from -0.046875 to 0.046875
- queries: bfloat16 [8, 4096, 4096], P('blk', 'ex'), may hold values from -0.03125 to 0.03125
Outputs:
- scores: float32 [128, 4096], P('blk', 'ex')
All inputs are finite; a program needn't handle non-finite values.
Results may differ from a plain program's by a relative error of at most 0.005.
Values may be sent and summed in bfloat16 or wider, within the bound.
A program may use at most 64 MiB of HBM per device.

v0:
```python
import jax
import jax.numpy as jnp
from jax import lax
from jax.sharding import PartitionSpec as P


def shards(acts, out_grads, proj_in, proj_out, queries):
    seqs = acts.shape[1]
    tokens = acts.shape[2]
    rows_in = acts[0].reshape(seqs * tokens, acts.shape[3])
    rows_out = out_grads[0].reshape(seqs * tokens, out_grads.shape[3])
    in_low = lax.dot_general(
        rows_in, proj_in[0], (((1,), (1,)), ((), ())), preferred_element_type=jnp.float32
    ).astype(jnp.bfloat16)
    out_low = lax.dot_general(
        rows_out, proj_out[0], (((1,), (1,)), ((), ())), preferred_element_type=jnp.float32
    ).astype(jnp.bfloat16)
    in_low = in_low.reshape(seqs, tokens, -1)
    out_low = out_low.reshape(seqs, tokens, -1)
    outer = jnp.einsum("itr,its->irs", in_low, out_low, preferred_element_type=jnp.float32)
    grads = outer.reshape(seqs, -1).astype(jnp.bfloat16)
    query_rows = queries[0]
    gathered = lax.all_gather(grads, "ex", axis=0, tiled=True)
    partial_scores = lax.dot_general(
        gathered, query_rows, (((1,), (1,)), ((), ())), preferred_element_type=jnp.float32
    )
    summed = lax.psum(partial_scores, "blk")
    share_rows = summed.shape[0] // lax.axis_size("blk")
    first_row = lax.axis_index("blk") * share_rows
    return lax.dynamic_slice_in_dim(summed, first_row, share_rows, 0)


def solution(mesh):
    placed = (
        P("blk", "ex", None, None),
        P("blk", "ex", None, None),
        P("blk", None, None),
        P("blk", None, None),
        P("blk", "ex", None),
    )
    return jax.shard_map(
        shards, mesh=mesh, in_specs=placed, out_specs=P("blk", "ex"), check_vma=False
    )
```

profile of v0, /device:TPU:4, one launch (start us, length us, event | category | flops | bytes accessed | tf_op | source)
XLA Modules:
  0.0 181.6 jit_solution(13350242231525435015)
XLA Ops:
  6.5 0.0 copy-start
  6.5 0.0 all-gather.3.cloned.1.call-start
  6.5 0.0 copy-start.1
  6.5 6.1 %fusion.2 = bf16[256,64]{0,1:T(8,128)(2,1)S(1)} fusion(bf16[256,14336]{1,0:T(8,128)(2,1)} %bitcast.21, bf16[1,64,14336]{2,1,0:T(8,128)(2,1)} %param.8), kind=kOutput, calls=%fused_computation.3 | convolution fusion | flops 469778432 | bytes 9207808 | tf_op jit(solution)/shard_map/dot_general | solution.py:15
  12.6 0.1 copy.10
  12.7 0.0 copy-done
  12.8 0.0 copy-done.1
  12.8 0.8 convolution_convert_fusion.1
  13.5 0.1 reshape.8
  13.6 0.1 convolution_convert_fusion
  13.8 0.7 reshape.10
  14.5 0.0 all-gather.3.cloned.1.call-update
  14.5 0.0 all-reduce.2.cloned.1.call-start
  14.6 78.8 %all-gather.3.cloned.1.call-done = bf16[32,4,4096]{2,1,0:T(4,128)(2,1)} async-done(((bf16[1,4,4096]{2,1,0:T(4,128)(2,1)}), bf16[32,4,4096]{2,1,0:T(4,128)(2,1)}) %all-gather.3.cloned.1.call-update) | async-done | bytes 1048592 | tf_op jit(solution)/shard_map/all_gather | solution.py:23
  93.3 1.3 reshape.11
  94.7 2.3 %fusion.5 = f32[128,128]{1,0:T(8,128)} fusion(bf16[128,4096]{1,0:T(8,128)(2,1)S(1)} %reshape.11, bf16[1,128,4096]{2,1,0:T(8,128)(2,1)} %param.9), kind=kOutput, calls=%fused_computation.5 | convolution fusion | flops 134217728 | bytes 2162688 | tf_op jit(solution)/shard_map/dot_general | solution.py:24
  97.0 0.0 all-reduce.2.cloned.1.call-update
  97.0 76.4 %all-reduce.2.cloned.1.call-done = f32[128,128]{1,0:T(8,128)} async-done(((f32[128,128]{1,0:T(8,128)}), f32[128,128]{1,0:T(8,128)}) %all-reduce.2.cloned.1.call-update) | async-done | bytes 65552 | tf_op jit(solution)/shard_map/psum | solution.py:27
  173.4 1.3 constant_dynamic-slice_fusion
Async XLA Ops:
  6.5 6.2 %copy-start = (bf16[1,4,64,4096]{3,2,1,0:T(8,128)(2,1)S(1)}, bf16[1,4,64,4096]{3,2,1,0:T(8,128)(2,1)}, u32[]{:S(2)}) copy-start(bf16[1,4,64,4096]{3,2,1,0:T(8,128)(2,1)} %param.5) | copy-start | bytes 6291460
  6.5 86.8 %all-gather.3.cloned.1.call-start = ((), (), s32[]{:S(2)}) async-start(), calls=%async_computation.1 | async-start | bytes 1081344 | tf_op jit(solution)/shard_map/all_gather | solution.py:23
  6.5 6.2 %copy-start.1 = (bf16[1,64,4096]{2,1,0:T(8,128)(2,1)S(1)}, bf16[1,64,4096]{2,1,0:T(8,128)(2,1)}, u32[]{:S(2)}) copy-start(bf16[1,64,4096]{2,1,0:T(8,128)(2,1)} %param.7) | copy-start | bytes 1572868
  14.5 158.9 %all-reduce.2.cloned.1.call-start = ((), (), s32[]{:S(2)}) async-start(), calls=%async_computation | async-start | bytes 131072 | tf_op jit(solution)/shard_map/psum | solution.py:27
Sparse Core Ops, SparseCore 0:
  14.7 78.6 all-gather.2
  97.1 76.2 all-reduce.1
where the time goes:
time: 182 us
  waiting for transfers between devices  155 us (85%)
  between operations  13.4 us (7%)
  matrix products  9.27 us (5%)
  local copies, waits for them, and re-layouts  3.59 us (2%)
    all_gather x1, waiting for transfers between devices, shards(): gathered = lax.all_gather(grads, 'ex', axis=0, tiled=True)  78.8 us
    psum x1, waiting for transfers between devices, shards(): summed = lax.psum(partial_scores, 'blk')  76.4 us
    dot_general x1, matrix products, shards(): lax.dot_general(rows_out, proj_out[0], (((1,), (1,)), ((), ())), preferre...  6.08 us
  transfers between devices with their start and end apart: 2, of which 2 were waited for; matrix products, arithmetic and copies ran while one was open for 0% of the time, Pallas kernels for 0%

commit v1 on v0

v1 whole, which is shorter than its diff:
```python
import jax
import jax.numpy as jnp
from jax import lax
from jax.experimental import pallas as pl
from jax.experimental.pallas import tpu as pltpu
from jax.sharding import PartitionSpec as P

MESH = pl.DeviceIdType.MESH
NZ = 8
NB = 8
EX = 4
TOK = 64
RANK = 64
J = RANK * RANK // 128
NT = (((1,), (1,)), ((), ()))


def slice_at(k):
    if isinstance(k, int):
        return (k + 1) // 2 if k % 2 else (NZ - k // 2) % NZ
    return jnp.where(lax.rem(k, 2) == 1, (k + 1) // 2, lax.rem(NZ - k // 2, NZ))


def kernel(
    acts, outg, pin, pout, q, out,
    vacts, voutg, vpin, vpout, vq, inf, eo, gbuf, fs, part,
    asem, osem, wsem, zss, zrs, xss, xrs, css, crs, rss, rrs, lsem,
):
    ex, blk = lax.axis_index("ex"), lax.axis_index("blk")
    z, xh, core = ex // 4, lax.rem(ex // 2, 2), lax.rem(ex, 2)

    def at(z_, x_, c_):
        return (z_ * 4 + x_ * 2 + c_, blk)

    x_peer = at(z, 1 - xh, core)
    c_peer = at(z, xh, 1 - core)

    load_pin = pltpu.make_async_copy(pin, vpin, wsem.at[0])
    load_pout = pltpu.make_async_copy(pout, vpout, wsem.at[1])
    load_q = pltpu.make_async_copy(q, vq, wsem.at[2])
    load_acts = pltpu.make_async_copy(acts, vacts, asem)

    def load_outg(i):
        return pltpu.make_async_copy(outg.at[i], voutg.at[i], osem.at[i])

    load_pin.start()
    load_acts.start()
    load_pout.start()
    for i in range(EX):
        load_outg(i).start()
    load_q.start()

    barrier = pltpu.get_barrier_semaphore()
    for d in range(1, NZ):
        pl.semaphore_signal(barrier, inc=1, device_id=at(lax.rem(z + d, NZ), xh, core), device_id_type=MESH)
    pl.semaphore_signal(barrier, inc=1, device_id=x_peer, device_id_type=MESH)
    pl.semaphore_signal(barrier, inc=1, device_id=c_peer, device_id_type=MESH)
    for d in range(1, NB):
        pl.semaphore_signal(barrier, inc=1, device_id=(ex, lax.rem(blk + d, NB)), device_id_type=MESH)

    load_pin.wait()
    load_acts.wait()
    low = lax.dot_general(vpin[...], vacts[...], NT, preferred_element_type=jnp.float32)
    low = low.astype(jnp.bfloat16).astype(jnp.float32)
    for h in range(2):
        inf[:, h, :] = low[:, h * 128:(h + 1) * 128]
    for h in range(2):
        for odd in range(2):
            eo[odd * (RANK // 2):(odd + 1) * (RANK // 2), h * 128:(h + 1) * 128] = (
                inf[pl.ds(odd, RANK // 2, stride=2), h, :].astype(jnp.bfloat16)
            )
    load_pout.wait()
    pl.semaphore_wait(barrier, NZ - 1 + 2 + NB - 1)

    def z_copy(d, i):
        return pltpu.make_async_remote_copy(
            src_ref=gbuf.at[0, core, xh, i],
            dst_ref=gbuf.at[NZ - d, core, xh, i],
            send_sem=zss.at[d, i],
            recv_sem=zrs.at[NZ - d, i],
            device_id=at(lax.rem(z + d, NZ), xh, core),
            device_id_type=MESH,
        )

    def x_copy(dz, x_):
        return pltpu.make_async_remote_copy(
            src_ref=gbuf.at[dz, core, x_],
            dst_ref=gbuf.at[dz, core, x_],
            send_sem=xss.at[dz],
            recv_sem=xrs.at[dz],
            device_id=x_peer,
            device_id_type=MESH,
        )

    def c_copy(dz, c_):
        return pltpu.make_async_remote_copy(
            src_ref=gbuf.at[dz, c_],
            dst_ref=gbuf.at[dz, c_],
            send_sem=css.at[dz],
            recv_sem=crs.at[dz],
            device_id=c_peer,
            device_id_type=MESH,
        )

    lane = lax.broadcasted_iota(jnp.int32, (RANK, EX * TOK), 1)

    @pl.loop(0, EX)
    def _(i):
        load_outg(i).wait()
        low = lax.dot_general(voutg[i], vpout[...], NT, preferred_element_type=jnp.float32)
        low = low.astype(jnp.bfloat16)
        mine = jnp.where(lane // TOK == i, eo[...], jnp.zeros_like(eo))
        g = jnp.dot(mine, jnp.concatenate([low] * EX, axis=0), preferred_element_type=jnp.float32)
        g = jnp.concatenate([g[:J], g[J:]], axis=1)
        gbuf[0, core, xh, i] = g.astype(jnp.bfloat16)
        for d in (4, 3, 5, 2, 6, 1, 7):
            z_copy(d, i).start()

    load_q.wait()

    def r_copy(dz, keeper):
        return pltpu.make_async_remote_copy(
            src_ref=part.at[dz],
            dst_ref=out.at[blk],
            send_sem=rss.at[dz],
            recv_sem=rrs.at[blk],
            device_id=(ex, keeper),
            device_id_type=MESH,
        )

    def l_copy(dz):
        return pltpu.make_async_copy(part.at[dz], out.at[blk], lsem)

    @pl.loop(0, NZ + 2)
    def _(k):
        @pl.when(k < NZ)
        def _():
            dz = slice_at(k)

            @pl.when(k > 0)
            def _():
                for i in range(EX):
                    pltpu.make_async_copy(gbuf.at[dz, core, xh, i], gbuf.at[dz, core, xh, i], zrs.at[dz, i]).wait()

            x_copy(dz, xh).start()

        @pl.when(jnp.logical_and(k >= 1, k < NZ + 1))
        def _():
            dz = slice_at(k - 1)
            x_copy(dz, 1 - xh).wait_recv()
            c_copy(dz, core).start()

        @pl.when(k >= 2)
        def _():
            dz = slice_at(k - 2)
            c_copy(dz, 1 - core).wait_recv()
            for x_ in range(2):
                for c_ in range(2):
                    for i in range(EX):
                        row = (x_ * 2 + c_) * EX + i
                        fs[row * J:(row + 1) * J, :] = gbuf[dz, c_, x_, i].astype(jnp.float32)
            rows = jnp.concatenate(
                [fs[pl.ds(j, 16, stride=J), :].astype(jnp.bfloat16) for j in range(J)], axis=1
            )
            part[dz] = lax.dot_general(rows, vq[...], NT, preferred_element_type=jnp.float32)
            keeper = lax.rem(z + dz, NB)

            @pl.when(keeper == blk)
            def _():
                l_copy(dz).start()

            @pl.when(keeper != blk)
            def _():
                r_copy(dz, keeper).start()

    @pl.loop(0, NZ)
    def _(dz):
        @pl.when(dz > 0)
        def _():
            for i in range(EX):
                z_copy(dz, i).wait_send()

        x_copy(dz, xh).wait_send()
        c_copy(dz, core).wait_send()
        keeper = lax.rem(z + dz, NB)

        @pl.when(keeper == blk)
        def _():
            l_copy(dz).wait()

        @pl.when(keeper != blk)
        def _():
            r_copy(dz, keeper).wait_send()

    @pl.loop(0, NB)
    def _(s):
        @pl.when(s != blk)
        def _():
            pltpu.make_async_copy(out.at[s], out.at[s], rrs.at[s]).wait()


def shards(acts, out_grads, proj_in, proj_out, queries):
    d, ff = acts.shape[3], out_grads.shape[3]
    nq, nk = queries.shape[1:]
    bf16, f32 = jnp.bfloat16, jnp.float32
    dma = pltpu.SemaphoreType.DMA
    terms = pl.pallas_call(
        kernel,
        out_shape=jax.ShapeDtypeStruct((NB, 16, nq), f32),
        in_specs=[pl.BlockSpec(memory_space=pl.ANY)] * 5,
        out_specs=pl.BlockSpec(memory_space=pl.ANY),
        scratch_shapes=[
            pltpu.VMEM((EX * TOK, d), bf16),
            pltpu.VMEM((EX, TOK, ff), bf16),
            pltpu.VMEM((RANK, d), bf16),
            pltpu.VMEM((RANK, ff), bf16),
            pltpu.VMEM((nq, nk), bf16),
            pltpu.VMEM((RANK, 2, 128), f32),
            pltpu.VMEM((RANK, EX * TOK), bf16),
            pltpu.VMEM((NZ, 2, 2, EX, J, 128), bf16),
            pltpu.VMEM((16 * J, 128), f32),
            pltpu.VMEM((NZ, 16, nq), f32),
            dma,
            dma((EX,)),
            dma((3,)),
            dma((NZ, EX)),
            dma((NZ, EX)),
            dma((NZ,)),
            dma((NZ,)),
            dma((NZ,)),
            dma((NZ,)),
            dma((NZ,)),
            dma((NB,)),
            dma,
        ],
        compiler_params=pltpu.CompilerParams(
            collective_id=0, has_side_effects=True, vmem_limit_bytes=60 * 1024 * 1024
        ),
        name="scores",
    )(
        acts.reshape(EX * TOK, d),
        out_grads[0],
        proj_in[0],
        proj_out[0],
        queries[0],
    )
    return jnp.sum(terms, axis=0)


def solution(mesh):
    placed = (
        P("blk", "ex", None, None),
        P("blk", "ex", None, None),
        P("blk", None, None),
        P("blk", None, None),
        P("blk", "ex", None),
    )
    return jax.shard_map(
        shards, mesh=mesh, in_specs=placed, out_specs=P("blk", "ex"), check_vma=False
    )
```

time: 182 us -> 40.5 us (0.22)
  the two profiles are of different devices: /device:TPU:4 before, /device:TPU:3 now
where the time goes in v1:
time: 40.5 us; the launch traced here: 40.4 us
  Pallas kernels  38.9 us (96%)
  other arithmetic  1.45 us (4%)
    pallas_call x1, Pallas kernels, shards(): pl.pallas_call(kernel, out_shape=jax.ShapeDtypeStruct((NB, 16, nq), f32),...  38.9 us
    reduce_sum x1, other arithmetic, shards(): return jnp.sum(terms, axis=0)  1.45 us

profile of v1, /device:TPU:3, one launch (start us, length us, event | category | flops | bytes accessed | tf_op | source)
XLA Modules:
  0.0 40.4 jit_solution(11585210319602638763)
XLA Ops:
  0.0 38.9 %scores.1 = f32[8,16,128]{2,1,0:T(8,128)} custom-call(bf16[256,4096]{1,0:T(8,128)(2,1)} %bitcast.6, bf16[4,64,14336]{2,1,0:T(8,128)(2,1)} %bitcast.5, bf16[64,4096]{1,0:T(8,128)(2,1)} %bitcast.9, bf16[64,14336]{1,0:T(8,128)(2,1)} %bitcast.7, bf16[128,4096]{1,0:T(8,128)(2,1)} %bitcast.8), custom_call_target="tpu_custom_call" | custom-call | tf_op jit(solution)/shard_map/scores/pallas_call | solution.py:207
  38.9 1.4 %reduce_sum.9 = f32[16,128]{1,0:T(8,128)} reduce(f32[8,16,128]{2,1,0:T(8,128)} %scores.1, f32[]{:T(128)} %constant.0.clone.1), dimensions={0}, to_apply=%region_0.0 | reduce | flops 14336 | bytes 73732 | tf_op jit(solution)/shard_map/reduce_sum | solution.py:247

commit v2 on v1

v2 whole, which is shorter than its diff:
```python
import jax
import jax.numpy as jnp
from jax import lax
from jax.experimental import pallas as pl
from jax.experimental.pallas import tpu as pltpu
from jax.sharding import PartitionSpec as P

MESH = pl.DeviceIdType.MESH
NZ = 8
NB = 8
NEAR = (2, -2, 1, -1)
EX = 4
TOK = 64
RANK = 64
J = RANK * RANK // 128
NT = (((1,), (1,)), ((), ()))


def kernel(
    acts, outg, pin, pout, q, out,
    vacts, voutg, vpin, vpout, vq, inf, eo, gbuf, fs, part,
    asem, osem, wsem, xss, xrs, zss, zrs, dss, drs, fss, frs, hss, hrs, css, crs, rss, rrs, lsem,
):
    ex, blk = lax.axis_index("ex"), lax.axis_index("blk")
    z, xh, core = ex // 4, lax.rem(ex // 2, 2), lax.rem(ex, 2)

    def at(dz, x_, c_):
        return (lax.rem(z + dz + NZ, NZ) * 4 + x_ * 2 + c_, blk)

    x_peer = at(0, 1 - xh, core)
    c_peer = at(0, xh, 1 - core)

    load_pin = pltpu.make_async_copy(pin, vpin, wsem.at[0])
    load_pout = pltpu.make_async_copy(pout, vpout, wsem.at[1])
    load_q = pltpu.make_async_copy(q, vq, wsem.at[2])
    load_acts = pltpu.make_async_copy(acts, vacts, asem)

    def load_outg(i):
        return pltpu.make_async_copy(outg.at[i], voutg.at[i], osem.at[i])

    load_pin.start()
    load_acts.start()
    load_pout.start()
    load_outg(0).start()

    barrier = pltpu.get_barrier_semaphore()
    peers = [x_peer, c_peer]
    peers += [at(dz, x_, core) for dz in NEAR for x_ in range(2)]
    peers += [(ex, lax.rem(blk + d, NB)) for d in range(1, NB)]
    for peer in peers:
        pl.semaphore_signal(barrier, inc=1, device_id=peer, device_id_type=MESH)

    load_pin.wait()
    load_acts.wait()
    load_outg(1).start()
    load_outg(2).start()
    low = lax.dot_general(vpin[...], vacts[...], NT, preferred_element_type=jnp.float32)
    low = low.astype(jnp.bfloat16).astype(jnp.float32)
    for h in range(2):
        inf[:, h, :] = low[:, h * 128:(h + 1) * 128]
    for h in range(2):
        for odd in range(2):
            eo[odd * (RANK // 2):(odd + 1) * (RANK // 2), h * 128:(h + 1) * 128] = (
                inf[pl.ds(odd, RANK // 2, stride=2), h, :].astype(jnp.bfloat16)
            )
    load_pout.wait()
    load_outg(3).start()
    pl.semaphore_wait(barrier, len(peers))

    def remote(src, dst, send_sem, recv_sem, device):
        return pltpu.make_async_remote_copy(
            src_ref=src, dst_ref=dst, send_sem=send_sem, recv_sem=recv_sem,
            device_id=device, device_id_type=MESH,
        )

    def x_copy(i):
        block = gbuf.at[0, core, i, xh]
        return remote(block, block, xss.at[i], xrs.at[i], x_peer)

    def z_copy(d, i):
        there = (NZ - d) % NZ
        return remote(
            gbuf.at[0, core, i, xh], gbuf.at[there, core, i, xh],
            zss.at[there, i], zrs.at[there, i], at(d, xh, core),
        )

    def d_copy(d, i):
        there = (NZ - d) % NZ
        return remote(
            gbuf.at[0, core, i, xh], gbuf.at[there, core, i, xh],
            dss.at[there, i], drs.at[there, i], at(d, 1 - xh, core),
        )

    def f_copy(d, i):
        here, there = (NZ - 2 * d) % NZ, (NZ - 3 * d) % NZ
        return remote(
            gbuf.at[here, core, i], gbuf.at[there, core, i],
            fss.at[there, i], frs.at[there, i], at(d, xh, core),
        )

    def h_copy(d, i):
        here, col = (NZ - 2 * d) % NZ, 0 if d > 0 else 1
        return remote(
            gbuf.at[here, core, i, col], gbuf.at[NZ // 2, core, i, col],
            hss.at[col, i], hrs.at[col, i], at(2 * d, xh, core),
        )

    def c_copy(dz, c_):
        block = gbuf.at[dz, c_]
        return remote(block, block, css.at[dz], crs.at[dz], c_peer)

    def arrived(ref, sem):
        pltpu.make_async_copy(ref, ref, sem).wait()

    lane = lax.broadcasted_iota(jnp.int32, (RANK, EX * TOK), 1)

    @pl.loop(0, EX)
    def _(i):
        load_outg(i).wait()

        @pl.when(i == 0)
        def _():
            load_q.start()

        low = lax.dot_general(voutg[i], vpout[...], NT, preferred_element_type=jnp.float32)
        low = low.astype(jnp.bfloat16)
        mine = jnp.where(lane // TOK == i, eo[...], jnp.zeros_like(eo))
        g = jnp.dot(mine, jnp.concatenate([low] * EX, axis=0), preferred_element_type=jnp.float32)
        g = jnp.concatenate([g[:J], g[J:]], axis=1)
        gbuf[0, core, i, xh] = g.astype(jnp.bfloat16)
        for d in NEAR:
            d_copy(d, i).start()
            z_copy(d, i).start()
        x_copy(i).start()

    @pl.loop(0, EX)
    def _(i):
        for dz, d in ((6, 1), (2, -1)):
            arrived(gbuf.at[dz, core, i, 0], zrs.at[dz, i])
            arrived(gbuf.at[dz, core, i, 0], drs.at[dz, i])
            h_copy(d, i).start()
            f_copy(d, i).start()

    for i in range(EX):
        arrived(gbuf.at[0, core, i, 0], xrs.at[i])
        for dz in (1, 7):
            arrived(gbuf.at[dz, core, i, 0], zrs.at[dz, i])
            arrived(gbuf.at[dz, core, i, 0], drs.at[dz, i])
    for dz in (1, 7, 2, 6, 0):
        c_copy(dz, core).start()
    load_q.wait()

    def r_copy(dz, keeper):
        return remote(part.at[dz], out.at[blk], rss.at[dz], rrs.at[blk], (ex, keeper))

    def l_copy(dz):
        return pltpu.make_async_copy(part.at[dz], out.at[blk], lsem)

    @pl.loop(1, NZ // 2 + 1)
    def _(t):
        pair = (t, jnp.where(t == NZ // 2, 0, NZ - t))
        for n, dz in enumerate(pair):
            c_copy(dz, 1 - core).wait_recv()
            for x_ in range(2):
                for c_ in range(2):
                    for i in range(EX):
                        row = ((n * 2 + x_) * 2 + c_) * EX + i
                        fs[row * J:(row + 1) * J, :] = gbuf[dz, c_, i, x_].astype(jnp.float32)
        rows = jnp.concatenate(
            [fs[pl.ds(j, 32, stride=J), :].astype(jnp.bfloat16) for j in range(J)], axis=1
        )
        scores = lax.dot_general(rows, vq[...], NT, preferred_element_type=jnp.float32)
        for n, dz in enumerate(pair):
            part[dz] = scores[n * 16:(n + 1) * 16]
            keeper = lax.rem(z + dz, NB)

            @pl.when(keeper == blk)
            def _():
                l_copy(dz).start()

            @pl.when(keeper != blk)
            def _():
                r_copy(dz, keeper).start()

        @pl.when(t == 1)
        def _():
            for dz in (3, 5):
                for i in range(EX):
                    arrived(gbuf.at[dz, core, i], frs.at[dz, i])
                c_copy(dz, core).start()

        @pl.when(t == 2)
        def _():
            for i in range(EX):
                for col in range(2):
                    arrived(gbuf.at[4, core, i, col], hrs.at[col, i])
            c_copy(4, core).start()

    @pl.loop(0, EX)
    def _(i):
        for d in NEAR:
            d_copy(d, i).wait_send()
            z_copy(d, i).wait_send()
        x_copy(i).wait_send()
        for d in (1, -1):
            h_copy(d, i).wait_send()
            f_copy(d, i).wait_send()

    @pl.loop(0, NZ)
    def _(dz):
        c_copy(dz, core).wait_send()
        keeper = lax.rem(z + dz, NB)

        @pl.when(keeper == blk)
        def _():
            l_copy(dz).wait()

        @pl.when(keeper != blk)
        def _():
            r_copy(dz, keeper).wait_send()

        @pl.when(dz != blk)
        def _():
            arrived(out.at[dz], rrs.at[dz])


def shards(acts, out_grads, proj_in, proj_out, queries):
    d, ff = acts.shape[3], out_grads.shape[3]
    nq, nk = queries.shape[1:]
    bf16, f32 = jnp.bfloat16, jnp.float32
    dma = pltpu.SemaphoreType.DMA
    terms = pl.pallas_call(
        kernel,
        out_shape=jax.ShapeDtypeStruct((NB, 16, nq), f32),
        in_specs=[pl.BlockSpec(memory_space=pl.ANY)] * 5,
        out_specs=pl.BlockSpec(memory_space=pl.ANY),
        scratch_shapes=[
            pltpu.VMEM((EX * TOK, d), bf16),
            pltpu.VMEM((EX, TOK, ff), bf16),
            pltpu.VMEM((RANK, d), bf16),
            pltpu.VMEM((RANK, ff), bf16),
            pltpu.VMEM((nq, nk), bf16),
            pltpu.VMEM((RANK, 2, 128), f32),
            pltpu.VMEM((RANK, EX * TOK), bf16),
            pltpu.VMEM((NZ, 2, EX, 2, J, 128), bf16),
            pltpu.VMEM((32 * J, 128), f32),
            pltpu.VMEM((NZ, 16, nq), f32),
            dma,
            dma((EX,)),
            dma((3,)),
            dma((EX,)),
            dma((EX,)),
            dma((NZ, EX)),
            dma((NZ, EX)),
            dma((NZ, EX)),
            dma((NZ, EX)),
            dma((NZ, EX)),
            dma((NZ, EX)),
            dma((2, EX)),
            dma((2, EX)),
            dma((NZ,)),
            dma((NZ,)),
            dma((NZ,)),
            dma((NB,)),
            dma,
        ],
        compiler_params=pltpu.CompilerParams(
            collective_id=0, has_side_effects=True, vmem_limit_bytes=60 * 1024 * 1024
        ),
        name="scores",
    )(
        acts.reshape(EX * TOK, d),
        out_grads[0],
        proj_in[0],
        proj_out[0],
        queries[0],
    )
    return jnp.sum(terms, axis=0)


def solution(mesh):
    placed = (
        P("blk", "ex", None, None),
        P("blk", "ex", None, None),
        P("blk", None, None),
        P("blk", None, None),
        P("blk", "ex", None),
    )
    return jax.shard_map(
        shards, mesh=mesh, in_specs=placed, out_specs=P("blk", "ex"), check_vma=False
    )
```

time: 40.5 us -> 31.8 us (0.79)
  the two profiles are of different devices: /device:TPU:3 before, /device:TPU:1 now
where the time goes in v2:
time: 31.8 us; the launch traced here: 31.7 us
  Pallas kernels  30.2 us (95%)
  other arithmetic  1.45 us (5%)
    pallas_call x1, Pallas kernels, shards(): pl.pallas_call(kernel, out_shape=jax.ShapeDtypeStruct((NB, 16, nq), f32),...  30.2 us
    reduce_sum x1, other arithmetic, shards(): return jnp.sum(terms, axis=0)  1.45 us

profile of v2, /device:TPU:1, one launch (start us, length us, event | category | flops | bytes accessed | tf_op | source)
XLA Modules:
  0.0 31.7 jit_solution(3560151115557647748)
XLA Ops:
  0.0 30.2 %scores.1 = f32[8,16,128]{2,1,0:T(8,128)} custom-call(bf16[256,4096]{1,0:T(8,128)(2,1)} %bitcast.6, bf16[4,64,14336]{2,1,0:T(8,128)(2,1)} %bitcast.5, bf16[64,4096]{1,0:T(8,128)(2,1)} %bitcast.9, bf16[64,14336]{1,0:T(8,128)(2,1)} %bitcast.7, bf16[128,4096]{1,0:T(8,128)(2,1)} %bitcast.8), custom_call_target="tpu_custom_call" | custom-call | tf_op jit(solution)/shard_map/scores/pallas_call | solution.py:232
  30.2 1.4 %reduce_sum.9 = f32[16,128]{1,0:T(8,128)} reduce(f32[8,16,128]{2,1,0:T(8,128)} %scores.1, f32[]{:T(128)} %constant.0.clone.1), dimensions={0}, to_apply=%region_0.0 | reduce | flops 14336 | bytes 73732 | tf_op jit(solution)/shard_map/reduce_sum | solution.py:278

commit v3 on v2

v3 whole, which is shorter than its diff:
```python
import jax
import jax.numpy as jnp
from jax import lax
from jax.experimental import pallas as pl
from jax.experimental.pallas import tpu as pltpu
from jax.sharding import PartitionSpec as P

MESH = pl.DeviceIdType.MESH
NZ = 8
NB = 8
NEAR = (2, -2, 1, -1)
FAR = (4, 3, -3)
LAST = 3
EX = 4
TOK = 64
RANK = 64
J = RANK * RANK // 128
NT = (((1,), (1,)), ((), ()))


def kernel(
    acts, outg, pin, pout, q, out,
    vacts, voutg, vpin, vpout, vq, vqt, inf, gbuf, fs, part, terms,
    asem, osem, wsem, xss, xrs, zss, zrs, dss, drs, fss, frs, hss, hrs, qss, qrs, rss, rrs,
):
    ex, blk = lax.axis_index("ex"), lax.axis_index("blk")
    z, xh, core = ex // 4, lax.rem(ex // 2, 2), lax.rem(ex, 2)

    def at(dz, x_, c_):
        return (lax.rem(z + dz + NZ, NZ) * 4 + x_ * 2 + c_, blk)

    x_peer = at(0, 1 - xh, core)
    c_peer = at(0, xh, 1 - core)

    load_pin = pltpu.make_async_copy(pin, vpin, wsem.at[0])
    load_pout = pltpu.make_async_copy(pout, vpout, wsem.at[1])
    load_q = pltpu.make_async_copy(q, vq, wsem.at[2])

    def load_acts(i):
        return pltpu.make_async_copy(acts.at[i], vacts.at[i], asem.at[i])

    def load_outg(i):
        return pltpu.make_async_copy(outg.at[i], voutg.at[i], osem.at[i])

    load_pin.start()
    load_acts(0).start()
    load_pout.start()
    load_outg(0).start()

    barrier = pltpu.get_barrier_semaphore()
    peers = [x_peer, c_peer]
    peers += [at(dz, x_, core) for dz in NEAR + FAR for x_ in range(2)]
    peers += [(e, lax.rem(blk + d, NB)) for d in range(1, NB) for e in (ex, c_peer[0])]
    for peer in peers:
        pl.semaphore_signal(barrier, inc=1, device_id=peer, device_id_type=MESH)

    def remote(src, dst, send_sem, recv_sem, device):
        return pltpu.make_async_remote_copy(
            src_ref=src, dst_ref=dst, send_sem=send_sem, recv_sem=recv_sem,
            device_id=device, device_id_type=MESH,
        )

    def x_copy(i):
        block = gbuf.at[0, i, xh]
        return remote(block, block, xss.at[i], xrs.at[i], x_peer)

    def z_copy(d, i):
        there = (NZ - d) % NZ
        return remote(
            gbuf.at[0, i, xh], gbuf.at[there, i, xh],
            zss.at[there, i], zrs.at[there, i], at(d, xh, core),
        )

    def d_copy(d, i):
        there = (NZ - d) % NZ
        return remote(
            gbuf.at[0, i, xh], gbuf.at[there, i, xh],
            dss.at[there, i], drs.at[there, i], at(d, 1 - xh, core),
        )

    def f_copy(d, i):
        here, there = (NZ - 2 * d) % NZ, (NZ - 3 * d) % NZ
        return remote(
            gbuf.at[here, i], gbuf.at[there, i],
            fss.at[there, i], frs.at[there, i], at(d, xh, core),
        )

    def h_copy(d, i):
        here, col = (NZ - 2 * d) % NZ, 0 if d > 0 else 1
        return remote(
            gbuf.at[here, i, col], gbuf.at[NZ // 2, i, col],
            hss.at[col, i], hrs.at[col, i], at(2 * d, xh, core),
        )

    q_copy = remote(vqt.at[core], vqt.at[core], qss, qrs, c_peer)

    def arrived(ref, sem):
        pltpu.make_async_copy(ref, ref, sem).wait()

    def direct(dz, i):
        arrived(gbuf.at[dz, i, 0], zrs.at[dz, i])
        arrived(gbuf.at[dz, i, 0], drs.at[dz, i])

    load_pin.wait()
    load_acts(1).start()
    load_outg(1).start()
    load_acts(0).wait()
    load_pout.wait()

    @pl.loop(0, EX)
    def _(i):
        @pl.when(i > 0)
        def _():
            load_acts(i).wait()

        load_outg(i).wait()

        @pl.when(i < EX - 2)
        def _():
            load_acts(i + 2).start()
            load_outg(i + 2).start()

        @pl.when(i == EX - 2)
        def _():
            load_q.start()

        tall = lax.dot_general(vpin[...], vacts[i], NT, preferred_element_type=jnp.float32)
        inf[:, :TOK] = tall.astype(jnp.bfloat16).astype(jnp.float32)
        low = lax.dot_general(voutg[i], vpout[...], NT, preferred_element_type=jnp.float32)
        split = jnp.concatenate(
            [inf[pl.ds(odd, RANK // 2, stride=2), :][:, :TOK] for odd in range(2)], axis=0
        )
        g = jnp.dot(
            split.astype(jnp.bfloat16), low.astype(jnp.bfloat16), preferred_element_type=jnp.float32
        )
        g = jnp.concatenate([g[:J], g[J:]], axis=1)
        gbuf[0, i, xh] = g.astype(jnp.bfloat16)

        @pl.when(i == 0)
        def _():
            pl.semaphore_wait(barrier, len(peers))

        @pl.when(i >= LAST)
        def _():
            for d in FAR:
                d_copy(d, i).start()
                z_copy(d, i).start()

        for d in NEAR:
            d_copy(d, i).start()
            z_copy(d, i).start()
        x_copy(i).start()

    load_q.wait()

    @pl.loop(0, max(LAST, 2))
    def _(i):
        @pl.when(i < 2)
        def _():
            @pl.loop(0, J // 2)
            def _(j):
                k = pl.multiple_of((i * (J // 2) + j) * 128, 128)
                vqt[core, pl.ds(k, 128), :] = vq[:, pl.ds(k, 128)].T

        @pl.when(i == 1)
        def _():
            q_copy.start()

        @pl.when(i < LAST)
        def _():
            for dz, d in ((6, 1), (2, -1)):
                direct(dz, i)
                h_copy(d, i).start()
                f_copy(d, i).start()

    def r_copy(dz, c_, keeper):
        return remote(
            part.at[dz, c_], terms.at[core, blk], rss.at[dz, c_], rrs.at[core, blk],
            (ex - core + c_, keeper),
        )

    def elsewhere(c_, keeper):
        return jnp.logical_or(keeper != blk, c_ != core)

    @pl.loop(0, NZ // 2 + 1)
    def _(t):
        single = lax.rem(t, NZ // 2) == 0
        pair = (t, jnp.where(single, t, NZ - t))

        @pl.when(t == 0)
        def _():
            for i in range(EX):
                arrived(gbuf.at[0, i, 0], xrs.at[i])
            arrived(vqt.at[0], qrs)

        @pl.when(t == 1)
        def _():
            for i in range(EX):
                direct(1, i)
                direct(7, i)

        @pl.when(t == 2)
        def _():
            for i in range(LAST, EX):
                direct(2, i)
                direct(6, i)

        @pl.when(t == 3)
        def _():
            for dz in (3, 5):
                for i in range(EX):
                    if i < LAST:
                        arrived(gbuf.at[dz, i], frs.at[dz, i])
                    else:
                        direct(dz, i)

        @pl.when(t == 4)
        def _():
            for i in range(EX):
                if i < LAST:
                    for col in range(2):
                        arrived(gbuf.at[4, i, col], hrs.at[col, i])
                else:
                    direct(4, i)

        for n, dz in enumerate(pair):
            for x_ in range(2):
                for i in range(EX):
                    row = (n * 2 + x_) * EX + i
                    fs[row * J:(row + 1) * J, :] = gbuf[dz, i, x_].astype(jnp.float32)
        rows = jnp.concatenate(
            [fs[pl.ds(j, 16, stride=J), :].astype(jnp.bfloat16) for j in range(J)], axis=1
        )
        scores = jnp.dot(
            rows, jnp.concatenate([vqt[0], vqt[1]], axis=1), preferred_element_type=jnp.float32
        )

        def finish(n):
            dz = pair[n]
            keeper = lax.rem(z + dz, NB)
            nq = scores.shape[1] // 2
            for c_ in range(2):
                block = scores[n * 8:(n + 1) * 8, c_ * nq:(c_ + 1) * nq]

                @pl.when(elsewhere(c_, keeper))
                def _():
                    part[dz, c_] = block
                    r_copy(dz, c_, keeper).start()

                @pl.when(jnp.logical_not(elsewhere(c_, keeper)))
                def _():
                    terms[core, blk] = block

        finish(0)

        @pl.when(jnp.logical_not(single))
        def _():
            finish(1)

    q_copy.wait_send()

    @pl.loop(0, EX)
    def _(i):
        for d in NEAR:
            d_copy(d, i).wait_send()
            z_copy(d, i).wait_send()
        x_copy(i).wait_send()

        @pl.when(i < LAST)
        def _():
            for d in (1, -1):
                h_copy(d, i).wait_send()
                f_copy(d, i).wait_send()

        @pl.when(i >= LAST)
        def _():
            for d in FAR:
                d_copy(d, i).wait_send()
                z_copy(d, i).wait_send()

    @pl.loop(0, NZ)
    def _(dz):
        keeper = lax.rem(z + dz, NB)
        for c_ in range(2):
            @pl.when(elsewhere(c_, keeper))
            def _():
                r_copy(dz, c_, keeper).wait_send()

            @pl.when(jnp.logical_or(dz != blk, c_ != core))
            def _():
                arrived(terms.at[c_, dz], rrs.at[c_, dz])

    for c_ in range(2):
        total = jnp.sum(terms[c_], axis=0)
        for x_ in range(2):
            row = (x_ * 2 + c_) * EX
            out[row:row + EX, :] = total[x_ * EX:(x_ + 1) * EX]


def shards(acts, out_grads, proj_in, proj_out, queries):
    d, ff = acts.shape[3], out_grads.shape[3]
    nq, nk = queries.shape[1:]
    bf16, f32 = jnp.bfloat16, jnp.float32
    dma = pltpu.SemaphoreType.DMA
    return pl.pallas_call(
        kernel,
        out_shape=pltpu.VMEM((16, nq), f32),
        in_specs=[pl.BlockSpec(memory_space=pl.ANY)] * 5,
        out_specs=pl.BlockSpec(memory_space=pltpu.VMEM),
        scratch_shapes=[
            pltpu.VMEM((EX, TOK, d), bf16),
            pltpu.VMEM((EX, TOK, ff), bf16),
            pltpu.VMEM((RANK, d), bf16),
            pltpu.VMEM((RANK, ff), bf16),
            pltpu.VMEM((nq, nk), bf16),
            pltpu.VMEM((2, nk, nq), bf16),
            pltpu.VMEM((RANK, 128), f32),
            pltpu.VMEM((NZ, EX, 2, J, 128), bf16),
            pltpu.VMEM((16 * J, 128), f32),
            pltpu.VMEM((NZ, 2, 8, nq), f32),
            pltpu.VMEM((2, NB, 8, nq), f32),
            dma((EX,)),
            dma((EX,)),
            dma((3,)),
            dma((EX,)),
            dma((EX,)),
            dma((NZ, EX)),
            dma((NZ, EX)),
            dma((NZ, EX)),
            dma((NZ, EX)),
            dma((NZ, EX)),
            dma((NZ, EX)),
            dma((2, EX)),
            dma((2, EX)),
            dma,
            dma,
            dma((NZ, 2)),
            dma((2, NB)),
        ],
        compiler_params=pltpu.CompilerParams(
            collective_id=0, has_side_effects=True, vmem_limit_bytes=60 * 1024 * 1024
        ),
        name="scores",
    )(acts[0], out_grads[0], proj_in[0], proj_out[0], queries[0])


def solution(mesh):
    placed = (
        P("blk", "ex", None, None),
        P("blk", "ex", None, None),
        P("blk", None, None),
        P("blk", None, None),
        P("blk", "ex", None),
    )
    return jax.shard_map(
        shards, mesh=mesh, in_specs=placed, out_specs=P("blk", "ex"), check_vma=False
    )
```

time: 31.8 us -> 28.6 us (0.90)
  the two profiles are of different devices: /device:TPU:1 before, /device:TPU:3 now
where the time goes in v3:
time: 28.6 us; the launch traced here: 28.5 us
  Pallas kernels  27.9 us (98%)
  local copies, waits for them, and re-layouts  0.6 us (2%)
    pallas_call x1, Pallas kernels, shards(): pl.pallas_call(kernel, out_shape=pltpu.VMEM((16, nq), f32), in_specs=[pl....  27.9 us
    unnamed x1, local copies, waits for them, and re-layouts  0.6 us

profile of v3, /device:TPU:3, one launch (start us, length us, event | category | flops | bytes accessed | tf_op | source)
XLA Modules:
  0.0 28.5 jit_solution(8135780256722303185)
XLA Ops:
  0.0 27.9 %scores.1 = f32[16,128]{1,0:T(8,128)S(1)} custom-call(bf16[4,64,4096]{2,1,0:T(8,128)(2,1)} %bitcast.6, bf16[4,64,14336]{2,1,0:T(8,128)(2,1)} %bitcast.5, bf16[64,4096]{1,0:T(8,128)(2,1)} %bitcast.9, bf16[64,14336]{1,0:T(8,128)(2,1)} %bitcast.7, bf16[128,4096]{1,0:T(8,128)(2,1)} %bitcast.8), custom_call_target="tpu_custom_call" | custom-call | tf_op jit(solution)/shard_map/scores/pallas_call | solution.py:305
  27.9 0.6 %copy.7 = f32[16,128]{1,0:T(8,128)} copy(f32[16,128]{1,0:T(8,128)S(1)} %scores.1) | data formatting | bytes 16384

commit v4 on v3

--- a/solution.py
+++ b/solution.py
@@ -9,7 +9,7 @@
 NZ = 8
 NB = 8
 NEAR = (2, -2, 1, -1)
-FAR = (4, 3, -3)
+FAR = (4,)
 LAST = 3
 EX = 4
 TOK = 64
@@ -20,7 +20,7 @@
 
 def kernel(
     acts, outg, pin, pout, q, out,
-    vacts, voutg, vpin, vpout, vq, vqt, inf, gbuf, fs, part, terms,
+    vacts, voutg, vpin, vpout, vq, inf, gbuf, fs, part, terms,
     asem, osem, wsem, xss, xrs, zss, zrs, dss, drs, fss, frs, hss, hrs, qss, qrs, rss, rrs,
 ):
     ex, blk = lax.axis_index("ex"), lax.axis_index("blk")
@@ -34,7 +34,7 @@
 
     load_pin = pltpu.make_async_copy(pin, vpin, wsem.at[0])
     load_pout = pltpu.make_async_copy(pout, vpout, wsem.at[1])
-    load_q = pltpu.make_async_copy(q, vq, wsem.at[2])
+    load_q = pltpu.make_async_copy(q, vq.at[core], wsem.at[2])
 
     def load_acts(i):
         return pltpu.make_async_copy(acts.at[i], vacts.at[i], asem.at[i])
@@ -92,7 +92,7 @@
             hss.at[col, i], hrs.at[col, i], at(2 * d, xh, core),
         )
 
-    q_copy = remote(vqt.at[core], vqt.at[core], qss, qrs, c_peer)
+    q_copy = remote(q, vq.at[core], qss, qrs, c_peer)
 
     def arrived(ref, sem):
         pltpu.make_async_copy(ref, ref, sem).wait()
@@ -151,27 +151,22 @@
             z_copy(d, i).start()
         x_copy(i).start()
 
+        @pl.when(i == 0)
+        def _():
+            q_copy.start()
+
+    @pl.loop(0, EX)
+    def _(i):
+        for dz, d in ((6, 1), (2, -1)):
+            direct(dz, i)
+
+            @pl.when(i < LAST)
+            def _():
+                h_copy(d, i).start()
+
+            f_copy(d, i).start()
+
     load_q.wait()
-
-    @pl.loop(0, max(LAST, 2))
-    def _(i):
-        @pl.when(i < 2)
-        def _():
-            @pl.loop(0, J // 2)
-            def _(j):
-                k = pl.multiple_of((i * (J // 2) + j) * 128, 128)
-                vqt[core, pl.ds(k, 128), :] = vq[:, pl.ds(k, 128)].T
-
-        @pl.when(i == 1)
-        def _():
-            q_copy.start()
-
-        @pl.when(i < LAST)
-        def _():
-            for dz, d in ((6, 1), (2, -1)):
-                direct(dz, i)
-                h_copy(d, i).start()
-                f_copy(d, i).start()
 
     def r_copy(dz, c_, keeper):
         return remote(
@@ -182,61 +177,42 @@
     def elsewhere(c_, keeper):
         return jnp.logical_or(keeper != blk, c_ != core)
 
-    @pl.loop(0, NZ // 2 + 1)
+    @pl.loop(0, 2)
     def _(t):
-        single = lax.rem(t, NZ // 2) == 0
-        pair = (t, jnp.where(single, t, NZ - t))
+        slots = (4 * t, 1 + 2 * t, 7 - 2 * t, 2 + 4 * t)
 
         @pl.when(t == 0)
         def _():
             for i in range(EX):
                 arrived(gbuf.at[0, i, 0], xrs.at[i])
-            arrived(vqt.at[0], qrs)
-
-        @pl.when(t == 1)
-        def _():
-            for i in range(EX):
                 direct(1, i)
                 direct(7, i)
-
-        @pl.when(t == 2)
-        def _():
-            for i in range(LAST, EX):
-                direct(2, i)
-                direct(6, i)
-
-        @pl.when(t == 3)
-        def _():
-            for dz in (3, 5):
-                for i in range(EX):
-                    if i < LAST:
-                        arrived(gbuf.at[dz, i], frs.at[dz, i])
-                    else:
-                        direct(dz, i)
-
-        @pl.when(t == 4)
+            arrived(vq.at[0], qrs)
+
+        @pl.when(t == 1)
         def _():
             for i in range(EX):
+                for dz in (3, 5):
+                    arrived(gbuf.at[dz, i], frs.at[dz, i])
                 if i < LAST:
                     for col in range(2):
                         arrived(gbuf.at[4, i, col], hrs.at[col, i])
                 else:
                     direct(4, i)
 
-        for n, dz in enumerate(pair):
+        for n, dz in enumerate(slots):
             for x_ in range(2):
                 for i in range(EX):
                     row = (n * 2 + x_) * EX + i
                     fs[row * J:(row + 1) * J, :] = gbuf[dz, i, x_].astype(jnp.float32)
         rows = jnp.concatenate(
-            [fs[pl.ds(j, 16, stride=J), :].astype(jnp.bfloat16) for j in range(J)], axis=1
-        )
-        scores = jnp.dot(
-            rows, jnp.concatenate([vqt[0], vqt[1]], axis=1), preferred_element_type=jnp.float32
-        )
+            [fs[pl.ds(j, 32, stride=J), :].astype(jnp.bfloat16) for j in range(J)], axis=1
+        )
+        both = jnp.concatenate([vq[0], vq[1]], axis=0)
+        scores = lax.dot_general(rows, both, NT, preferred_element_type=jnp.float32)
 
         def finish(n):
-            dz = pair[n]
+            dz = slots[n]
             keeper = lax.rem(z + dz, NB)
             nq = scores.shape[1] // 2
             for c_ in range(2):
@@ -251,11 +227,8 @@
                 def _():
                     terms[core, blk] = block
 
-        finish(0)
-
-        @pl.when(jnp.logical_not(single))
-        def _():
-            finish(1)
+        for n in range(len(slots)):
+            finish(n)
 
     q_copy.wait_send()
 
@@ -266,11 +239,13 @@
             z_copy(d, i).wait_send()
         x_copy(i).wait_send()
 
+        for d in (1, -1):
+            f_copy(d, i).wait_send()
+
         @pl.when(i < LAST)
         def _():
             for d in (1, -1):
                 h_copy(d, i).wait_send()
-                f_copy(d, i).wait_send()
 
         @pl.when(i >= LAST)
         def _():
@@ -312,11 +287,10 @@
             pltpu.VMEM((EX, TOK, ff), bf16),
             pltpu.VMEM((RANK, d), bf16),
             pltpu.VMEM((RANK, ff), bf16),
-            pltpu.VMEM((nq, nk), bf16),
-            pltpu.VMEM((2, nk, nq), bf16),
+            pltpu.VMEM((2, nq, nk), bf16),
             pltpu.VMEM((RANK, 128), f32),
             pltpu.VMEM((NZ, EX, 2, J, 128), bf16),
-            pltpu.VMEM((16 * J, 128), f32),
+            pltpu.VMEM((32 * J, 128), f32),
             pltpu.VMEM((NZ, 2, 8, nq), f32),
             pltpu.VMEM((2, NB, 8, nq), f32),
             dma((EX,)),

time: 28.6 us -> 28.6 us (level)
  no operation moved by 1% of the time
where the time goes in v4:
time: 28.6 us; the launch traced here: 28.5 us
  Pallas kernels  27.9 us (98%)
  local copies, waits for them, and re-layouts  0.6 us (2%)
    pallas_call x1, Pallas kernels, shards(): pl.pallas_call(kernel, out_shape=pltpu.VMEM((16, nq), f32), in_specs=[pl....  27.9 us
    unnamed x1, local copies, waits for them, and re-layouts  0.6 us

profile of v4, /device:TPU:3, one launch (start us, length us, event | category | flops | bytes accessed | tf_op | source)
XLA Modules:
  0.0 28.5 jit_solution(16514069748326224745)
XLA Ops:
  0.0 27.9 %scores.1 = f32[16,128]{1,0:T(8,128)S(1)} custom-call(bf16[4,64,4096]{2,1,0:T(8,128)(2,1)} %bitcast.6, bf16[4,64,14336]{2,1,0:T(8,128)(2,1)} %bitcast.5, bf16[64,4096]{1,0:T(8,128)(2,1)} %bitcast.9, bf16[64,14336]{1,0:T(8,128)(2,1)} %bitcast.7, bf16[128,4096]{1,0:T(8,128)(2,1)} %bitcast.8), custom_call_target="tpu_custom_call" | custom-call | tf_op jit(solution)/shard_map/scores/pallas_call | solution.py:280
  27.9 0.6 %copy.7 = f32[16,128]{1,0:T(8,128)} copy(f32[16,128]{1,0:T(8,128)S(1)} %scores.1) | data formatting | bytes 16384
